TPU v7x, 512 devices: a whole 4x4x16 slice. The times are simulated.
512 devices in a mesh: dp: 8 (over y, core), seq: 64 (over x, z).
Axes of the slice: x: 4, y: 4, z: 16, core: 2. Of those that a mesh axis runs over, the one named last changes fastest.
Arguments:
- queries: bfloat16 [8, 16384, 384], P('dp', 'seq'), may hold values from -6 to 6
- keys: bfloat16 [8, 16384, 384], P('dp', 'seq'), may hold values from -6 to 6
- values: bfloat16 [8, 16384, 384], P('dp', 'seq'), may hold values from -6 to 6
- outputs: bfloat16 [8, 16384, 384], P('dp', 'seq'), may hold values from -16 to 16
- d_final: bfloat16 [8, 16384, 768], P('dp', 'seq'), may hold values from -6 to 6
- stats: float32 [8, 16384, 8], P('dp', 'seq'), may hold values from 6.5 to 8
- w_out: bfloat16 [384, 768], replicated, may hold values from -0.21875 to 0.21875
Outputs:
- d_queries: bfloat16 [8, 16384, 384], P('dp', 'seq')
- d_keys: bfloat16 [8, 16384, 384], P('dp', 'seq')
- d_values: bfloat16 [8, 16384, 384], P('dp', 'seq')
- grad_weight: float32 [384, 768], P('seq')
All inputs are finite; a program needn't handle non-finite values.
Results may differ from a plain program's by a relative error of at most 0.0057.
Values may be sent and summed in bfloat16 or wider, within the bound.
No kernel may reach another device: no remote copies, remote signals or barrier semaphores. Data moves between devices by JAX's collectives and lax.ppermute only.
A program may use at most 64 MiB of HBM per device.

v0:
```python
import jax
import jax.numpy as jnp
from jax import lax
from jax.sharding import PartitionSpec as P

GROUP = 8


def swapped(shard, axis, distance):
    return lax.ppermute(shard, axis, [(i, i ^ 1 << distance) for i in range(lax.axis_size(axis))])


def pick(x, stride, heads):
    shaped = x.reshape(x.shape[0] // stride, stride, heads, x.shape[-1])
    return jnp.stack([shaped[:, h % stride, h, :] for h in range(heads)], axis=1)


def place(y, stride, heads, rows):
    shaped = jnp.zeros((rows // stride, stride, heads, y.shape[-1]), jnp.float32)
    for h in range(heads):
        shaped = shaped.at[:, h % stride, h, :].set(y[:, h, :])
    return shaped.reshape(rows, heads, y.shape[-1])


def set_backward(query, d_out, lse, delta, keys, values, scale):
    scores = jnp.einsum("nhc,mhc->hnm", query, keys, preferred_element_type=jnp.float32) * scale
    probs = jnp.exp(scores - jnp.transpose(lse)[:, :, None])
    d_probs = jnp.einsum("nhc,mhc->hnm", d_out, values, preferred_element_type=jnp.float32)
    d_scores = (probs * (d_probs - jnp.transpose(delta)[:, :, None])).astype(jnp.bfloat16)
    probs_low = probs.astype(jnp.bfloat16)
    d_query = jnp.einsum("hnm,mhc->nhc", d_scores, keys, preferred_element_type=jnp.float32) * scale
    d_key = jnp.einsum("hnm,nhc->mhc", d_scores, query, preferred_element_type=jnp.float32) * scale
    d_value = jnp.einsum("hnm,nhc->mhc", probs_low, d_out, preferred_element_type=jnp.float32)
    return (d_query, d_key, d_value)


def group_collect(block, bits):
    where = lax.axis_index("seq")
    gathered = block
    for bit in range(bits):
        other = swapped(gathered, "seq", bit)
        high = where >> bit & 1
        gathered = jnp.where(
            high == 1,
            jnp.concatenate([other, gathered], axis=1),
            jnp.concatenate([gathered, other], axis=1),
        )
    return gathered


def group_return(grads, bits):
    where = lax.axis_index("seq")
    current = grads
    for bit in reversed(range(bits)):
        half = current.shape[1] // 2
        lower = current[:, :half]
        upper = current[:, half:]
        high = where >> bit & 1
        keep = jnp.where(high == 1, upper, lower)
        send = jnp.where(high == 1, lower, upper)
        current = keep + swapped(send, "seq", bit)
    return current


def on_device(queries, keys, values, outputs, d_final, stats, w_out):
    query2 = queries[0]
    key2 = keys[0]
    value2 = values[0]
    output2 = outputs[0]
    upstream = d_final[0]
    lse = stats[0]
    rows = query2.shape[0]
    width = query2.shape[1]
    heads = lse.shape[1]
    size = width // heads
    scale = float(size) ** (-0.5)
    seq_count = lax.axis_size("seq")
    d_out = lax.dot_general(
        upstream, w_out, (((1,), (1,)), ((), ())), preferred_element_type=jnp.float32
    ).astype(jnp.bfloat16)
    query3 = query2.reshape(rows, heads, size)
    key3 = key2.reshape(rows, heads, size)
    value3 = value2.reshape(rows, heads, size)
    dout3 = d_out.reshape(rows, heads, size)
    delta = jnp.sum(
        dout3.astype(jnp.float32) * output2.reshape(rows, heads, size).astype(jnp.float32), axis=-1
    )
    full = lax.dot_general(
        output2, upstream, (((0,), (0,)), ((), ())), preferred_element_type=jnp.float32
    )
    summed = lax.psum(full, "dp")
    grad_weight = lax.psum_scatter(summed, "seq", scatter_dimension=0, tiled=True)
    dq0, dk0, dv0 = set_backward(query3, dout3, lse, delta, key3, value3, scale)
    total_q = dq0
    total_k = dk0
    total_v = dv0

    def level_inputs(stride):
        return (
            pick(query3, stride, heads),
            pick(dout3, stride, heads),
            pick(lse[:, :, None], stride, heads)[..., 0],
            pick(delta[:, :, None], stride, heads)[..., 0],
            pick(key3, stride, heads),
            pick(value3, stride, heads),
        )

    group_bits = GROUP.bit_length() - 1
    pq, pd, pl, pdl, pk, pv = level_inputs(GROUP)
    count = rows // GROUP
    pair = jnp.stack([pk.reshape(count, width), pv.reshape(count, width)])
    remote = group_collect(pair, group_bits)
    dq1, dk1, dv1 = set_backward(
        pq,
        pd,
        pl,
        pdl,
        remote[0].reshape(-1, heads, size),
        remote[1].reshape(-1, heads, size),
        scale,
    )
    back = group_return(jnp.stack([dk1.reshape(-1, width), dv1.reshape(-1, width)]), group_bits)
    total_q = total_q + place(dq1, GROUP, heads, rows)
    total_k = total_k + place(back[0].reshape(count, heads, size), GROUP, heads, rows)
    total_v = total_v + place(back[1].reshape(count, heads, size), GROUP, heads, rows)
    fq, fd, fl, fdl, fk, fv = level_inputs(seq_count)
    far_count = rows // seq_count
    far_pair = jnp.stack([fk.reshape(far_count, width), fv.reshape(far_count, width)])
    far_remote = lax.all_gather(far_pair, "seq", axis=1, tiled=True)
    dq2, dk2, dv2 = set_backward(
        fq,
        fd,
        fl,
        fdl,
        far_remote[0].reshape(-1, heads, size),
        far_remote[1].reshape(-1, heads, size),
        scale,
    )
    far_terms = jnp.stack([dk2.reshape(-1, width), dv2.reshape(-1, width)])
    far_back = lax.psum_scatter(far_terms, "seq", scatter_dimension=1, tiled=True)
    total_q = total_q + place(dq2, seq_count, heads, rows)
    total_k = total_k + place(far_back[0].reshape(far_count, heads, size), seq_count, heads, rows)
    total_v = total_v + place(far_back[1].reshape(far_count, heads, size), seq_count, heads, rows)
    d_queries = total_q.reshape(1, rows, width).astype(jnp.bfloat16)
    d_keys = total_k.reshape(1, rows, width).astype(jnp.bfloat16)
    d_values = total_v.reshape(1, rows, width).astype(jnp.bfloat16)
    return (d_queries, d_keys, d_values, grad_weight)


def solution(mesh):
    placed = (
        P("dp", "seq", None),
        P("dp", "seq", None),
        P("dp", "seq", None),
        P("dp", "seq", None),
        P("dp", "seq", None),
        P("dp", "seq", None),
        P(),
    )
    return jax.shard_map(
        on_device,
        mesh=mesh,
        in_specs=placed,
        out_specs=(
            P("dp", "seq", None),
            P("dp", "seq", None),
            P("dp", "seq", None),
            P("seq", None),
        ),
        check_vma=False,
    )
```

profile of v0, /device:TPU:8, one launch (start us, length us, event | category | flops | bytes accessed | tf_op | source)
XLA Modules:
  0.0 632.5 jit_solution(2512236024374545083)
XLA Ops:
  8.8 158.2 %fusion = f32[8,768]{1,0:T(8,128)} fusion(f32[384,768]{1,0:T(8,128)S(1)} %fusion.28), kind=kCustom, calls=%all-reduce-scatter | all-reduce-scatter fusion | flops 393217 | bytes 1206272
  181.1 98.5 %all_gather.3 = bf16[2,256,384]{2,0,1:T(2,128)(2,1)S(1)} all-gather(bf16[2,4,384]{2,0,1:T(2,128)(2,1)S(1)} %copy.1023), channel_id=1, replica_groups=mesh['dp'=8,'seq'=64] {'seq'}, dimensions={1}, use_global_device_ids=true | all-gather | bytes 399360 | tf_op jit(solution)/shard_map/all_gather | solution.py:129
  298.7 3.0 collective-permute-start.21
  303.2 4.5 collective-permute-start.16
  307.8 9.6 %collective-permute-start.15 = (f32[8,768]{1,0:T(8,128)}, f32[8,768]{1,0:T(8,128)S(1)}, u32[]{:S(2)}, u32[]{:S(2)}) collective-permute-start(f32[8,768]{1,0:T(8,128)} %fusion), channel_id=1, source_target_pairs={{0,10},{1,11},{2,12},{3,13},{4,14},{5,15},{6,16},{7,17},{8,18},{9,... | collective-permute-start | bytes 73736
  317.4 2.6 collective-permute-start.1
  320.7 7.0 %collective-permute-start.14 = (f32[8,768]{1,0:T(8,128)}, f32[8,768]{1,0:T(8,128)S(1)}, u32[]{:S(2)}, u32[]{:S(2)}) collective-permute-start(f32[8,768]{1,0:T(8,128)} %fusion), channel_id=1, source_target_pairs={{0,9},{1,10},{2,11},{3,12},{4,13},{5,14},{6,15},{7,16},{8,17},{9,1... | collective-permute-start | bytes 73736
  327.7 7.8 %collective-permute-start.13 = (f32[8,768]{1,0:T(8,128)}, f32[8,768]{1,0:T(8,128)S(1)}, u32[]{:S(2)}, u32[]{:S(2)}) collective-permute-start(f32[8,768]{1,0:T(8,128)} %fusion), channel_id=1, source_target_pairs={{0,8},{1,9},{2,10},{3,11},{4,12},{5,13},{6,14},{7,15},{8,16},{9,17... | collective-permute-start | bytes 73736
  335.5 4.9 collective-permute-start.12
  340.4 8.4 %collective-permute-start.11 = (f32[8,768]{1,0:T(8,128)}, f32[8,768]{1,0:T(8,128)S(1)}, u32[]{:S(2)}, u32[]{:S(2)}) collective-permute-start(f32[8,768]{1,0:T(8,128)} %fusion), channel_id=1, source_target_pairs={{0,6},{1,7},{2,8},{3,9},{4,10},{5,11},{6,12},{7,13},{8,14},{9,15},... | collective-permute-start | bytes 73736
  348.9 6.3 collective-permute-start.10
  355.3 4.4 collective-permute-start.9
  359.7 3.4 collective-permute-start.8
  365.3 4.8 collective-permute-start.6
  375.8 2.4 reshape.1814
  380.2 23.5 %concatenate.120 = f32[134,768]{1,0:T(8,128)} concatenate(f32[6,768]{1,0:T(8,128)S(1)} %copy-done.23, f32[8,768]{1,0:T(8,128)} %collective-permute-done.20, f32[8,768]{1,0:T(8,128)} %collective-permute-done.19, f32[8,768]{1,0:T(8,128)} %collective-permute-done.18, f32[8,768]{1,0:T(8,128)} %collective-permute-done.17, f32[8,768]{1,0:T(8,128)S(1)} %copy-done.25, ...), dimensions={0} | concatenate | bytes 823296
  404.5 21.8 %psum.8 = f32[6,768]{1,0:T(8,128)} all-reduce(f32[6,768]{1,0:T(8,128)S(1)} %constant_dynamic-slice_fusion), channel_id=1, replica_groups=mesh['dp'=8,'seq'=64] {'dp'}, use_global_device_ids=true, to_apply=%region_2.0 | all-reduce | flops 4608 | bytes 36864 | tf_op jit(solution)/shard_map/psum | solution.py:91
  443.1 7.5 %collective-permute-start.3 = (f32[2,128,384]{2,1,0:T(8,128)}, f32[2,128,384]{2,1,0:T(8,128)}, u32[]{:S(2)}, u32[]{:S(2)}) collective-permute-start(f32[2,128,384]{2,1,0:T(8,128)} %broadcast_select_fusion), channel_id=1, source_target_pairs={{0,4},{1,5},{2,6},{3,7},{4,0},{5,1},{6,2},{7,3},{8,12},{9,13},{10,... | collective-permute-start | bytes 1179656 | tf_op jit(solution)/shard_map/ppermute | solution.py:10
  454.8 2.6 fusion.12
  459.2 24.2 %collective-permute-done.3 = f32[2,128,384]{2,1,0:T(8,128)} collective-permute-done((f32[2,128,384]{2,1,0:T(8,128)}, f32[2,128,384]{2,1,0:T(8,128)}, u32[]{:S(2)}, u32[]{:S(2)}) %collective-permute-start.3) | collective-permute-done | bytes 393248 | tf_op jit(solution)/shard_map/ppermute | solution.py:10
  488.0 97.0 %all-reduce.11.cloned.1.call-done = f32[2,256,384]{2,1,0:T(8,128)} async-done(((f32[2,256,384]{2,1,0:T(8,128)}), f32[2,256,384]{2,1,0:T(8,128)}) %all-reduce.11.cloned.1.call-update) | async-done | bytes 786448
  593.6 2.4 reshape.1832
  602.5 2.7 collective-permute-start.5
  619.2 2.4 fusion.11
  (412 shorter events, 105.6 us)
Async XLA Ops:
  7.2 169.2 %copy-start.13 = (bf16[1,256,384]{2,1,0:T(8,128)(2,1)S(1)}, bf16[1,256,384]{2,1,0:T(8,128)(2,1)}, u32[]{:S(2)}) copy-start(bf16[1,256,384]{2,1,0:T(8,128)(2,1)} %param.103) | copy-start | bytes 589828
  7.2 577.7 %all-reduce.11.cloned.1.call-start = ((), (), s32[]{:S(2)}) async-start(), calls=%async_computation | async-start | bytes 1572864
  167.0 140.7 %collective-permute-start.20 = (f32[8,768]{1,0:T(8,128)}, f32[8,768]{1,0:T(8,128)}, u32[]{:S(2)}, u32[]{:S(2)}) collective-permute-start(f32[8,768]{1,0:T(8,128)} %fusion), channel_id=1, source_target_pairs={{0,15},{1,16},{2,17},{3,18},{4,19},{5,20},{6,21},{7,22},{8,23},{9,... | collective-permute-start | bytes 73736
  168.9 148.5 %collective-permute-start.19 = (f32[8,768]{1,0:T(8,128)}, f32[8,768]{1,0:T(8,128)}, u32[]{:S(2)}, u32[]{:S(2)}) collective-permute-start(f32[8,768]{1,0:T(8,128)} %fusion), channel_id=1, source_target_pairs={{0,14},{1,15},{2,16},{3,17},{4,18},{5,19},{6,20},{7,21},{8,22},{9,... | collective-permute-start | bytes 73736
  170.8 149.9 %collective-permute-start.18 = (f32[8,768]{1,0:T(8,128)}, f32[8,768]{1,0:T(8,128)}, u32[]{:S(2)}, u32[]{:S(2)}) collective-permute-start(f32[8,768]{1,0:T(8,128)} %fusion), channel_id=1, source_target_pairs={{0,13},{1,14},{2,15},{3,16},{4,17},{5,18},{6,19},{7,20},{8,21},{9,... | collective-permute-start | bytes 73736
  172.7 155.0 %collective-permute-start.17 = (f32[8,768]{1,0:T(8,128)}, f32[8,768]{1,0:T(8,128)}, u32[]{:S(2)}, u32[]{:S(2)}) collective-permute-start(f32[8,768]{1,0:T(8,128)} %fusion), channel_id=1, source_target_pairs={{0,12},{1,13},{2,14},{3,15},{4,16},{5,17},{6,18},{7,19},{8,20},{9,... | collective-permute-start | bytes 73736
  288.9 9.8 %collective-permute-start = (bf16[2,32,384]{2,1,0:T(8,128)(2,1)}, bf16[2,32,384]{2,1,0:T(8,128)(2,1)}, u32[]{:S(2)}, u32[]{:S(2)}) collective-permute-start(bf16[2,32,384]{2,1,0:T(8,128)(2,1)} %constant_dynamic-update-slice_fusion.16), channel_id=1, source_target_pairs={{0,1},{1,0},{2,3},{3,2},{4,5},{5,4},{6,7},{7,6},{8,9},{9,8},{10,11... | collective-permute-start | bytes 147464 | tf_op jit(solution)/shard_map/ppermute | solution.py:10
  298.7 4.5 collective-permute-start.21
  303.2 32.2 %collective-permute-start.16 = (f32[8,768]{1,0:T(8,128)}, f32[8,768]{1,0:T(8,128)S(1)}, u32[]{:S(2)}, u32[]{:S(2)}) collective-permute-start(f32[8,768]{1,0:T(8,128)} %fusion), channel_id=1, source_target_pairs={{0,11},{1,12},{2,13},{3,14},{4,15},{5,16},{6,17},{7,18},{8,19},{9,... | collective-permute-start | bytes 73736
  307.8 32.6 %collective-permute-start.15 = (f32[8,768]{1,0:T(8,128)}, f32[8,768]{1,0:T(8,128)S(1)}, u32[]{:S(2)}, u32[]{:S(2)}) collective-permute-start(f32[8,768]{1,0:T(8,128)} %fusion), channel_id=1, source_target_pairs={{0,10},{1,11},{2,12},{3,13},{4,14},{5,15},{6,16},{7,17},{8,18},{9,... | collective-permute-start | bytes 73736
  317.4 31.4 %collective-permute-start.1 = (bf16[2,64,384]{2,1,0:T(8,128)(2,1)S(1)}, bf16[2,64,384]{2,1,0:T(8,128)(2,1)S(1)}, u32[]{:S(2)}, u32[]{:S(2)}) collective-permute-start(bf16[2,64,384]{2,1,0:T(8,128)(2,1)S(1)} %maximum_select_fusion.2), channel_id=1, source_target_pairs={{0,2},{1,3},{2,0},{3,1},{4,6},{5,7},{6,4},{7,5},{8,10},{9,11},{10,... | collective-permute-start | bytes 294920 | tf_op jit(solution)/shard_map/ppermute | solution.py:10
  320.7 34.6 %collective-permute-start.14 = (f32[8,768]{1,0:T(8,128)}, f32[8,768]{1,0:T(8,128)S(1)}, u32[]{:S(2)}, u32[]{:S(2)}) collective-permute-start(f32[8,768]{1,0:T(8,128)} %fusion), channel_id=1, source_target_pairs={{0,9},{1,10},{2,11},{3,12},{4,13},{5,14},{6,15},{7,16},{8,17},{9,1... | collective-permute-start | bytes 73736
  327.7 32.0 %collective-permute-start.13 = (f32[8,768]{1,0:T(8,128)}, f32[8,768]{1,0:T(8,128)S(1)}, u32[]{:S(2)}, u32[]{:S(2)}) collective-permute-start(f32[8,768]{1,0:T(8,128)} %fusion), channel_id=1, source_target_pairs={{0,8},{1,9},{2,10},{3,11},{4,12},{5,13},{6,14},{7,15},{8,16},{9,17... | collective-permute-start | bytes 73736
  335.5 27.7 %collective-permute-start.12 = (f32[8,768]{1,0:T(8,128)}, f32[8,768]{1,0:T(8,128)S(1)}, u32[]{:S(2)}, u32[]{:S(2)}) collective-permute-start(f32[8,768]{1,0:T(8,128)} %fusion), channel_id=1, source_target_pairs={{0,7},{1,8},{2,9},{3,10},{4,11},{5,12},{6,13},{7,14},{8,15},{9,16}... | collective-permute-start | bytes 73736
  340.4 24.9 %collective-permute-start.11 = (f32[8,768]{1,0:T(8,128)}, f32[8,768]{1,0:T(8,128)S(1)}, u32[]{:S(2)}, u32[]{:S(2)}) collective-permute-start(f32[8,768]{1,0:T(8,128)} %fusion), channel_id=1, source_target_pairs={{0,6},{1,7},{2,8},{3,9},{4,10},{5,11},{6,12},{7,13},{8,14},{9,15},... | collective-permute-start | bytes 73736
  348.9 21.3 %collective-permute-start.10 = (f32[8,768]{1,0:T(8,128)}, f32[8,768]{1,0:T(8,128)S(1)}, u32[]{:S(2)}, u32[]{:S(2)}) collective-permute-start(f32[8,768]{1,0:T(8,128)} %fusion), channel_id=1, source_target_pairs={{0,5},{1,6},{2,7},{3,8},{4,9},{5,10},{6,11},{7,12},{8,13},{9,14},{... | collective-permute-start | bytes 73736
  355.3 24.8 %collective-permute-start.9 = (f32[8,768]{1,0:T(8,128)}, f32[8,768]{1,0:T(8,128)}, u32[]{:S(2)}, u32[]{:S(2)}) collective-permute-start(f32[8,768]{1,0:T(8,128)} %fusion), channel_id=1, source_target_pairs={{0,4},{1,5},{2,6},{3,7},{4,8},{5,9},{6,10},{7,11},{8,12},{9,13},{1... | collective-permute-start | bytes 73736
  359.7 20.4 %collective-permute-start.8 = (f32[8,768]{1,0:T(8,128)}, f32[8,768]{1,0:T(8,128)}, u32[]{:S(2)}, u32[]{:S(2)}) collective-permute-start(f32[8,768]{1,0:T(8,128)} %fusion), channel_id=1, source_target_pairs={{0,3},{1,4},{2,5},{3,6},{4,7},{5,8},{6,9},{7,10},{8,11},{9,12},{10... | collective-permute-start | bytes 73736
  363.2 16.9 %collective-permute-start.7 = (f32[8,768]{1,0:T(8,128)}, f32[8,768]{1,0:T(8,128)}, u32[]{:S(2)}, u32[]{:S(2)}) collective-permute-start(f32[8,768]{1,0:T(8,128)} %fusion), channel_id=1, source_target_pairs={{0,2},{1,3},{2,4},{3,5},{4,6},{5,7},{6,8},{7,9},{8,10},{9,11},{10,... | collective-permute-start | bytes 73736
  365.3 14.8 %collective-permute-start.6 = (f32[8,768]{1,0:T(8,128)}, f32[8,768]{1,0:T(8,128)}, u32[]{:S(2)}, u32[]{:S(2)}) collective-permute-start(f32[8,768]{1,0:T(8,128)} %fusion), channel_id=1, source_target_pairs={{0,1},{1,2},{2,3},{3,4},{4,5},{5,6},{6,7},{7,8},{8,9},{9,10},{10,1... | collective-permute-start | bytes 73736
  370.2 56.1 %collective-permute-start.2 = (bf16[2,128,384]{2,1,0:T(8,128)(2,1)S(1)}, bf16[2,128,384]{2,1,0:T(8,128)(2,1)}, u32[]{:S(2)}, u32[]{:S(2)}) collective-permute-start(bf16[2,128,384]{2,1,0:T(8,128)(2,1)S(1)} %maximum_select_fusion.1), channel_id=1, source_target_pairs={{0,4},{1,5},{2,6},{3,7},{4,0},{5,1},{6,2},{7,3},{8,12},{9,13},{10,... | collective-permute-start | bytes 589832 | tf_op jit(solution)/shard_map/ppermute | solution.py:10
  443.1 40.3 %collective-permute-start.3 = (f32[2,128,384]{2,1,0:T(8,128)}, f32[2,128,384]{2,1,0:T(8,128)}, u32[]{:S(2)}, u32[]{:S(2)}) collective-permute-start(f32[2,128,384]{2,1,0:T(8,128)} %broadcast_select_fusion), channel_id=1, source_target_pairs={{0,4},{1,5},{2,6},{3,7},{4,0},{5,1},{6,2},{7,3},{8,12},{9,13},{10,... | collective-permute-start | bytes 1179656 | tf_op jit(solution)/shard_map/ppermute | solution.py:10
  486.1 114.7 %collective-permute-start.4 = (f32[2,64,384]{2,1,0:T(8,128)}, f32[2,64,384]{2,1,0:T(8,128)}, u32[]{:S(2)}, u32[]{:S(2)}) collective-permute-start(f32[2,64,384]{2,1,0:T(8,128)} %slice_select_fusion), channel_id=1, source_target_pairs={{0,2},{1,3},{2,0},{3,1},{4,6},{5,7},{6,4},{7,5},{8,10},{9,11},{10,... | collective-permute-start | bytes 589832 | tf_op jit(solution)/shard_map/ppermute | solution.py:10
  602.5 7.9 %collective-permute-start.5 = (f32[2,32,384]{2,1,0:T(8,128)S(1)}, f32[2,32,384]{2,1,0:T(8,128)S(1)}, u32[]{:S(2)}, u32[]{:S(2)}) collective-permute-start(f32[2,32,384]{2,1,0:T(8,128)S(1)} %slice_select_fusion.1), channel_id=1, source_target_pairs={{0,1},{1,0},{2,3},{3,2},{4,5},{5,4},{6,7},{7,6},{8,9},{9,8},{10,11... | collective-permute-start | bytes 294920 | tf_op jit(solution)/shard_map/ppermute | solution.py:10
  (43 other events, 1665.5 us)
Sparse Core Ops, SparseCore 0:
  286.1 298.8 all-reduce.10
where the time goes:
time: 636 us; the launch traced here: 633 us
  blocking collectives  279 us (44%)
  waiting for transfers between devices  122 us (19%)
  local copies, waits for them, and re-layouts  96.5 us (15%)
  starting transfers between devices  92.8 us (15%)
  matrix products  17.9 us (3%)
  between operations  16.9 us (3%)
  other arithmetic  8.05 us (1%)
    unnamed x1, blocking collectives  158 us
    all_gather x1, blocking collectives, on_device(): far_remote = lax.all_gather(far_pair, 'seq', axis=1, tiled=True)  98.5 us
    unnamed x18, waiting for transfers between devices  97.6 us
    unnamed x17, starting transfers between devices  74 us
    unnamed x208, local copies, waits for them, and re-layouts  38 us
    ppermute x6, waiting for transfers between devices, swapped(): lax.ppermute(shard, axis, [(i, i ^ 1 << distance) for i in range(lax.axis...  24.2 us
    scatter x54, local copies, waits for them, and re-layouts, place(): shaped = shaped.at[:, h % stride, h, :].set(y[:, h, :])  23.4 us
    psum x1, blocking collectives, on_device(): summed = lax.psum(full, 'dp')  21.8 us
  transfers between devices with their start and end apart: 23, of which 3 were waited for; matrix products, arithmetic and copies ran while one was open for 16% of the time, Pallas kernels for 0%

commit v1 on v0

--- a/solution.py
+++ b/solution.py
@@ -2,6 +2,7 @@
 import jax.numpy as jnp
 from jax import lax
 from jax.sharding import PartitionSpec as P
+from jax.lax import axis_size, ppermute
 
 GROUP = 8
 
@@ -88,7 +89,10 @@
     full = lax.dot_general(
         output2, upstream, (((0,), (0,)), ((), ())), preferred_element_type=jnp.float32
     )
-    summed = lax.psum(full, "dp")
+    cores_n = axis_size("dp")
+    summed = full
+    for m in [[(no, no ^ rr) for no in range(cores_n)] for rr in (1, 2, 4, 8, 16) if rr < cores_n]:
+        summed = summed + ppermute(summed, "dp", m)
     grad_weight = lax.psum_scatter(summed, "seq", scatter_dimension=0, tiled=True)
     dq0, dk0, dv0 = set_backward(query3, dout3, lse, delta, key3, value3, scale)
     total_q = dq0

time: 636 us -> 727 us (1.14)
  the two profiles are of different devices: /device:TPU:8 before, /device:TPU:32 now
where the time goes in v1:
time: 727 us; the launch traced here: 725 us
  blocking collectives  250 us (34%)
  waiting for transfers between devices  240 us (33%)
  starting transfers between devices  101 us (14%)
  local copies, waits for them, and re-layouts  83.8 us (12%)
  matrix products  18.3 us (3%)
  between operations  16.8 us (2%)
  other arithmetic  14.3 us (2%)
    unnamed x18, waiting for transfers between devices  180 us
    unnamed x1, blocking collectives  151 us
    all_gather x1, blocking collectives, on_device(): far_remote = lax.all_gather(far_pair, 'seq', axis=1, tiled=True)  99.4 us
    unnamed x17, starting transfers between devices  63.3 us
    ppermute x6, waiting for transfers between devices, swapped(): lax.ppermute(shard, axis, [(i, i ^ 1 << distance) for i in range(lax.axis...  38 us
    scatter x54, local copies, waits for them, and re-layouts, place(): shaped = shaped.at[:, h % stride, h, :].set(y[:, h, :])  28.5 us
    ppermute x6, starting transfers between devices, swapped(): lax.ppermute(shard, axis, [(i, i ^ 1 << distance) for i in range(lax.axis...  26.4 us
    ppermute x3, waiting for transfers between devices, on_device(): summed = summed + ppermute(summed, 'dp', m)  21.7 us
  transfers between devices with their start and end apart: 26, of which 6 were waited for; matrix products, arithmetic and copies ran while one was open for 13% of the time, Pallas kernels for 0%

profile of v1, /device:TPU:32, one launch (start us, length us, event | category | flops | bytes accessed | tf_op | source)
XLA Modules:
  0.0 724.9 jit_solution(1172852382626350500)
XLA Ops:
  16.5 99.4 %all_gather.3 = bf16[2,256,384]{2,0,1:T(2,128)(2,1)S(1)} all-gather(bf16[2,4,384]{2,0,1:T(2,128)(2,1)S(1)} %copy.1023), channel_id=1, replica_groups=mesh['dp'=8,'seq'=64] {'seq'}, dimensions={1}, use_global_device_ids=true | all-gather | bytes 399360 | tf_op jit(solution)/shard_map/all_gather | solution.py:133
  127.1 3.9 collective-permute-start
  144.7 3.7 collective-permute-start.1
  156.3 4.5 collective-permute-start.2
  161.4 16.7 %collective-permute-done.2 = bf16[2,128,384]{2,1,0:T(8,128)(2,1)S(1)} collective-permute-done((bf16[2,128,384]{2,1,0:T(8,128)(2,1)S(1)}, bf16[2,128,384]{2,1,0:T(8,128)(2,1)S(1)}, u32[]{:S(2)}, u32[]{:S(2)}) %collective-permute-start.2) | collective-permute-done | bytes 196640 | tf_op jit(solution)/shard_map/ppermute | solution.py:11
  199.6 2.6 fusion.12
  204.0 21.3 %collective-permute-done.3 = f32[2,128,384]{2,1,0:T(8,128)} collective-permute-done((f32[2,128,384]{2,1,0:T(8,128)}, f32[2,128,384]{2,1,0:T(8,128)}, u32[]{:S(2)}, u32[]{:S(2)}) %collective-permute-start.3) | collective-permute-done | bytes 393248 | tf_op jit(solution)/shard_map/ppermute | solution.py:11
  227.9 9.1 %collective-permute-start.4 = (f32[2,64,384]{2,1,0:T(8,128)}, f32[2,64,384]{2,1,0:T(8,128)}, u32[]{:S(2)}, u32[]{:S(2)}) collective-permute-start(f32[2,64,384]{2,1,0:T(8,128)} %slice_select_fusion), channel_id=1, source_target_pairs={{0,2},{1,3},{2,0},{3,1},{4,6},{5,7},{6,4},{7,5},{8,10},{9,11},{10,... | collective-permute-start | bytes 589832 | tf_op jit(solution)/shard_map/ppermute | solution.py:11
  237.0 180.1 %all-reduce.11.cloned.1.call-done = f32[2,256,384]{2,1,0:T(8,128)} async-done(((f32[2,256,384]{2,1,0:T(8,128)}), f32[2,256,384]{2,1,0:T(8,128)}) %all-reduce.11.cloned.1.call-update) | async-done | bytes 786448
  434.4 3.3 collective-permute-start.5
  443.0 2.8 add.157
  445.8 3.4 collective-permute-start.7
  451.5 15.9 %collective-permute-done.7 = f32[384,768]{1,0:T(8,128)} collective-permute-done((f32[384,768]{1,0:T(8,128)}, f32[384,768]{1,0:T(8,128)}, u32[]{:S(2)}, u32[]{:S(2)}) %collective-permute-start.7) | collective-permute-done | bytes 1179680 | tf_op jit(solution)/shard_map/ppermute | solution.py:95
  467.4 2.8 add.158
  470.2 6.0 collective-permute-start.8
  487.0 5.9 collective-permute-done.8
  494.6 151.1 %fusion = f32[8,768]{1,0:T(8,128)S(1)} fusion(f32[384,768]{1,0:T(8,128)S(1)} %add.159), kind=kCustom, calls=%all-reduce-scatter | all-reduce-scatter fusion | flops 393217 | bytes 1206272
  649.8 4.5 collective-permute-start.21
  657.0 16.0 %collective-permute-start.18 = (f32[8,768]{1,0:T(8,128)S(1)}, f32[8,768]{1,0:T(8,128)S(1)}, u32[]{:S(2)}, u32[]{:S(2)}) collective-permute-start(f32[8,768]{1,0:T(8,128)S(1)} %fusion), channel_id=1, source_target_pairs={{0,10},{1,11},{2,12},{3,13},{4,14},{5,15},{6,16},{7,17},{8,18},{9,... | collective-permute-start | bytes 73736
  676.9 11.2 %collective-permute-start.15 = (f32[8,768]{1,0:T(8,128)S(1)}, f32[8,768]{1,0:T(8,128)S(1)}, u32[]{:S(2)}, u32[]{:S(2)}) collective-permute-start(f32[8,768]{1,0:T(8,128)S(1)} %fusion), channel_id=1, source_target_pairs={{0,7},{1,8},{2,9},{3,10},{4,11},{5,12},{6,13},{7,14},{8,15},{9,16}... | collective-permute-start | bytes 73736
  692.6 6.3 collective-permute-start.13
  698.9 4.9 collective-permute-start.12
  705.5 4.5 collective-permute-start.10
  710.0 2.5 collective-permute-start.9
  (384 shorter events, 125.7 us)
Async XLA Ops:
  7.2 409.9 %all-reduce.11.cloned.1.call-start = ((), (), s32[]{:S(2)}) async-start(), calls=%async_computation | async-start | bytes 1572864
  127.1 16.7 %collective-permute-start = (bf16[2,32,384]{2,1,0:T(8,128)(2,1)}, bf16[2,32,384]{2,1,0:T(8,128)(2,1)}, u32[]{:S(2)}, u32[]{:S(2)}) collective-permute-start(bf16[2,32,384]{2,1,0:T(8,128)(2,1)} %constant_dynamic-update-slice_fusion.16), channel_id=1, source_target_pairs={{0,1},{1,0},{2,3},{3,2},{4,5},{5,4},{6,7},{7,6},{8,9},{9,8},{10,11... | collective-permute-start | bytes 147464 | tf_op jit(solution)/shard_map/ppermute | solution.py:11
  132.4 310.5 %collective-permute-start.6 = (f32[384,768]{1,0:T(8,128)}, f32[384,768]{1,0:T(8,128)}, u32[]{:S(2)}, u32[]{:S(2)}) collective-permute-start(f32[384,768]{1,0:T(8,128)} %fusion.28), channel_id=1, source_target_pairs={{0,64},{64,0},{128,192},{192,128},{256,320},{320,256},{384,448},{4... | collective-permute-start | bytes 3538952 | tf_op jit(solution)/shard_map/ppermute | solution.py:95
  144.7 11.5 %collective-permute-start.1 = (bf16[2,64,384]{2,1,0:T(8,128)(2,1)S(1)}, bf16[2,64,384]{2,1,0:T(8,128)(2,1)S(1)}, u32[]{:S(2)}, u32[]{:S(2)}) collective-permute-start(bf16[2,64,384]{2,1,0:T(8,128)(2,1)S(1)} %maximum_select_fusion.2), channel_id=1, source_target_pairs={{0,2},{1,3},{2,0},{3,1},{4,6},{5,7},{6,4},{7,5},{8,10},{9,11},{10,... | collective-permute-start | bytes 294920 | tf_op jit(solution)/shard_map/ppermute | solution.py:11
  156.3 21.8 %collective-permute-start.2 = (bf16[2,128,384]{2,1,0:T(8,128)(2,1)S(1)}, bf16[2,128,384]{2,1,0:T(8,128)(2,1)S(1)}, u32[]{:S(2)}, u32[]{:S(2)}) collective-permute-start(bf16[2,128,384]{2,1,0:T(8,128)(2,1)S(1)} %maximum_select_fusion.1), channel_id=1, source_target_pairs={{0,4},{1,5},{2,6},{3,7},{4,0},{5,1},{6,2},{7,3},{8,12},{9,13},{10,... | collective-permute-start | bytes 589832 | tf_op jit(solution)/shard_map/ppermute | solution.py:11
  193.6 31.7 %collective-permute-start.3 = (f32[2,128,384]{2,1,0:T(8,128)}, f32[2,128,384]{2,1,0:T(8,128)}, u32[]{:S(2)}, u32[]{:S(2)}) collective-permute-start(f32[2,128,384]{2,1,0:T(8,128)} %broadcast_select_fusion), channel_id=1, source_target_pairs={{0,4},{1,5},{2,6},{3,7},{4,0},{5,1},{6,2},{7,3},{8,12},{9,13},{10,... | collective-permute-start | bytes 1179656 | tf_op jit(solution)/shard_map/ppermute | solution.py:11
  227.9 204.8 %collective-permute-start.4 = (f32[2,64,384]{2,1,0:T(8,128)}, f32[2,64,384]{2,1,0:T(8,128)}, u32[]{:S(2)}, u32[]{:S(2)}) collective-permute-start(f32[2,64,384]{2,1,0:T(8,128)} %slice_select_fusion), channel_id=1, source_target_pairs={{0,2},{1,3},{2,0},{3,1},{4,6},{5,7},{6,4},{7,5},{8,10},{9,11},{10,... | collective-permute-start | bytes 589832 | tf_op jit(solution)/shard_map/ppermute | solution.py:11
  434.4 14.8 %collective-permute-start.5 = (f32[2,32,384]{2,1,0:T(8,128)S(1)}, f32[2,32,384]{2,1,0:T(8,128)S(1)}, u32[]{:S(2)}, u32[]{:S(2)}) collective-permute-start(f32[2,32,384]{2,1,0:T(8,128)S(1)} %slice_select_fusion.1), channel_id=1, source_target_pairs={{0,1},{1,0},{2,3},{3,2},{4,5},{5,4},{6,7},{7,6},{8,9},{9,8},{10,11... | collective-permute-start | bytes 294920 | tf_op jit(solution)/shard_map/ppermute | solution.py:11
  445.8 21.6 %collective-permute-start.7 = (f32[384,768]{1,0:T(8,128)}, f32[384,768]{1,0:T(8,128)}, u32[]{:S(2)}, u32[]{:S(2)}) collective-permute-start(f32[384,768]{1,0:T(8,128)} %add.157), channel_id=1, source_target_pairs={{0,128},{64,192},{128,0},{192,64},{256,384},{320,448},{384,256},{4... | collective-permute-start | bytes 3538952 | tf_op jit(solution)/shard_map/ppermute | solution.py:95
  470.2 22.6 %collective-permute-start.8 = (f32[384,768]{1,0:T(8,128)}, f32[384,768]{1,0:T(8,128)}, u32[]{:S(2)}, u32[]{:S(2)}) collective-permute-start(f32[384,768]{1,0:T(8,128)} %add.158), channel_id=1, source_target_pairs={{0,256},{64,320},{128,384},{192,448},{256,0},{320,64},{384,128},{4... | collective-permute-start | bytes 3538952 | tf_op jit(solution)/shard_map/ppermute | solution.py:95
  645.8 9.9 %collective-permute-start.24 = (f32[6,768]{1,0:T(8,128)S(1)}, f32[6,768]{1,0:T(8,128)S(1)}, u32[]{:S(2)}, u32[]{:S(2)}) collective-permute-start(f32[6,768]{1,0:T(8,128)S(1)} %slice.2078), channel_id=1, source_target_pairs={{0,16},{1,17},{2,18},{3,19},{4,20},{5,21},{6,22},{7,23},{8,24},{9,... | collective-permute-start | bytes 55304
  648.5 24.5 %collective-permute-start.22 = (f32[8,768]{1,0:T(8,128)S(1)}, f32[8,768]{1,0:T(8,128)S(1)}, u32[]{:S(2)}, u32[]{:S(2)}) collective-permute-start(f32[8,768]{1,0:T(8,128)S(1)} %fusion), channel_id=1, source_target_pairs={{0,14},{1,15},{2,16},{3,17},{4,18},{5,19},{6,20},{7,21},{8,22},{9,... | collective-permute-start | bytes 73736
  649.8 25.1 %collective-permute-start.21 = (f32[8,768]{1,0:T(8,128)S(1)}, f32[8,768]{1,0:T(8,128)S(1)}, u32[]{:S(2)}, u32[]{:S(2)}) collective-permute-start(f32[8,768]{1,0:T(8,128)S(1)} %fusion), channel_id=1, source_target_pairs={{0,13},{1,14},{2,15},{3,16},{4,17},{5,18},{6,19},{7,20},{8,21},{9,... | collective-permute-start | bytes 73736
  654.3 22.5 %collective-permute-start.20 = (f32[8,768]{1,0:T(8,128)S(1)}, f32[8,768]{1,0:T(8,128)S(1)}, u32[]{:S(2)}, u32[]{:S(2)}) collective-permute-start(f32[8,768]{1,0:T(8,128)S(1)} %fusion), channel_id=1, source_target_pairs={{0,12},{1,13},{2,14},{3,15},{4,16},{5,17},{6,18},{7,19},{8,20},{9,... | collective-permute-start | bytes 73736
  655.6 32.4 %collective-permute-start.19 = (f32[8,768]{1,0:T(8,128)S(1)}, f32[8,768]{1,0:T(8,128)S(1)}, u32[]{:S(2)}, u32[]{:S(2)}) collective-permute-start(f32[8,768]{1,0:T(8,128)S(1)} %fusion), channel_id=1, source_target_pairs={{0,11},{1,12},{2,13},{3,14},{4,15},{5,16},{6,17},{7,18},{8,19},{9,... | collective-permute-start | bytes 73736
  657.0 35.6 %collective-permute-start.18 = (f32[8,768]{1,0:T(8,128)S(1)}, f32[8,768]{1,0:T(8,128)S(1)}, u32[]{:S(2)}, u32[]{:S(2)}) collective-permute-start(f32[8,768]{1,0:T(8,128)S(1)} %fusion), channel_id=1, source_target_pairs={{0,10},{1,11},{2,12},{3,13},{4,14},{5,15},{6,16},{7,17},{8,18},{9,... | collective-permute-start | bytes 73736
  673.0 25.9 %collective-permute-start.17 = (f32[8,768]{1,0:T(8,128)S(1)}, f32[8,768]{1,0:T(8,128)S(1)}, u32[]{:S(2)}, u32[]{:S(2)}) collective-permute-start(f32[8,768]{1,0:T(8,128)S(1)} %fusion), channel_id=1, source_target_pairs={{0,9},{1,10},{2,11},{3,12},{4,13},{5,14},{6,15},{7,16},{8,17},{9,1... | collective-permute-start | bytes 73736
  674.9 28.9 %collective-permute-start.16 = (f32[8,768]{1,0:T(8,128)S(1)}, f32[8,768]{1,0:T(8,128)S(1)}, u32[]{:S(2)}, u32[]{:S(2)}) collective-permute-start(f32[8,768]{1,0:T(8,128)S(1)} %fusion), channel_id=1, source_target_pairs={{0,8},{1,9},{2,10},{3,11},{4,12},{5,13},{6,14},{7,15},{8,16},{9,17... | collective-permute-start | bytes 73736
  676.9 28.6 %collective-permute-start.15 = (f32[8,768]{1,0:T(8,128)S(1)}, f32[8,768]{1,0:T(8,128)S(1)}, u32[]{:S(2)}, u32[]{:S(2)}) collective-permute-start(f32[8,768]{1,0:T(8,128)S(1)} %fusion), channel_id=1, source_target_pairs={{0,7},{1,8},{2,9},{3,10},{4,11},{5,12},{6,13},{7,14},{8,15},{9,16}... | collective-permute-start | bytes 73736
  688.1 21.9 %collective-permute-start.14 = (f32[8,768]{1,0:T(8,128)S(1)}, f32[8,768]{1,0:T(8,128)S(1)}, u32[]{:S(2)}, u32[]{:S(2)}) collective-permute-start(f32[8,768]{1,0:T(8,128)S(1)} %fusion), channel_id=1, source_target_pairs={{0,6},{1,7},{2,8},{3,9},{4,10},{5,11},{6,12},{7,13},{8,14},{9,15},... | collective-permute-start | bytes 73736
  692.6 22.8 %collective-permute-start.13 = (f32[8,768]{1,0:T(8,128)S(1)}, f32[8,768]{1,0:T(8,128)S(1)}, u32[]{:S(2)}, u32[]{:S(2)}) collective-permute-start(f32[8,768]{1,0:T(8,128)S(1)} %fusion), channel_id=1, source_target_pairs={{0,5},{1,6},{2,7},{3,8},{4,9},{5,10},{6,11},{7,12},{8,13},{9,14},{... | collective-permute-start | bytes 73736
  698.9 16.5 %collective-permute-start.12 = (f32[8,768]{1,0:T(8,128)S(1)}, f32[8,768]{1,0:T(8,128)S(1)}, u32[]{:S(2)}, u32[]{:S(2)}) collective-permute-start(f32[8,768]{1,0:T(8,128)S(1)} %fusion), channel_id=1, source_target_pairs={{0,4},{1,5},{2,6},{3,7},{4,8},{5,9},{6,10},{7,11},{8,12},{9,13},{1... | collective-permute-start | bytes 73736
  703.8 11.6 %collective-permute-start.11 = (f32[8,768]{1,0:T(8,128)S(1)}, f32[8,768]{1,0:T(8,128)S(1)}, u32[]{:S(2)}, u32[]{:S(2)}) collective-permute-start(f32[8,768]{1,0:T(8,128)S(1)} %fusion), channel_id=1, source_target_pairs={{0,3},{1,4},{2,5},{3,6},{4,7},{5,8},{6,9},{7,10},{8,11},{9,12},{10... | collective-permute-start | bytes 73736
  705.5 10.0 %collective-permute-start.10 = (f32[8,768]{1,0:T(8,128)S(1)}, f32[8,768]{1,0:T(8,128)S(1)}, u32[]{:S(2)}, u32[]{:S(2)}) collective-permute-start(f32[8,768]{1,0:T(8,128)S(1)} %fusion), channel_id=1, source_target_pairs={{0,2},{1,3},{2,4},{3,5},{4,6},{5,7},{6,8},{7,9},{8,10},{9,11},{10,... | collective-permute-start | bytes 73736
  (28 other events, 571.3 us)
Sparse Core Ops, SparseCore 0:
  122.4 294.6 all-reduce.10
